TPU v7x, 32 devices: a whole 2x2x4 slice. The times are simulated.
32 devices in a mesh: rep: 2 (over y), expert: 8 (over z, x), group: 2 (over core).
Axes of the slice: x: 2, y: 2, z: 4, core: 2. Of those that a mesh axis runs over, the one named last changes fastest.
Arguments:
- tokens: bfloat16 [4096, 1024], P(('rep', 'expert', 'group')), parts along dimension 0, may hold values from -6 to 6
- w_gate: bfloat16 [16, 1024, 384], P('expert', 'group'), may hold values from -0.1875 to 0.1875
- w_up: bfloat16 [16, 1024, 384], P('expert', 'group'), may hold values from -0.1875 to 0.1875
- w_down: bfloat16 [16, 384, 1024], P('expert', 'group'), may hold values from -0.45927933 to 0.45927933
- route_ids: int32 [4096, 8], P(('rep', 'expert', 'group')), parts along dimension 0, may hold values from 0 to 15, all different within a row; in each aligned block of 128 rows (0 to 127, 128 to 255, ...) at most 80 rows name the same one
- route_scores: float32 [4096, 8], P(('rep', 'expert', 'group')), parts along dimension 0, may hold values from 0.05 to 1
- norm_gain: float32 [1024], replicated, may hold values from 0.5 to 1.5
- class_head: bfloat16 [1024, 2000], P(None, 'expert'), may hold values from -0.59765625 to 0.59765625
- targets: int32 [16, 2, 2000], P('rep', 'group', 'expert'), parts along dimension 0, may hold values 0 or 1
Outputs:
- token_grad: bfloat16 [4096, 1024], P(('rep', 'expert', 'group')), parts along dimension 0
- head_grad: float32 [2048, 2000], P('rep', 'expert'), parts along dimension 0
There are 2 independent parts, one for each index of `rep`. A program takes and returns all parts, laid end to end along the dimension named above; an argument that names none is the same for every part. Nothing has to cross between parts.
Inputs may be any that keep to these rules, and one draw needn't show every extreme that they name: `route_ids`: each row names 8 different experts; among the 128 tokens of one sequence no expert is named by more than 80 tokens, and in some sequences one expert is named by exactly 80.
All inputs are finite; a program needn't handle non-finite values. No bound on the sum of `targets` on one device may be relied on, other than what follows from the above.
Results may differ from a plain program's by a relative error of at most 0.022.
Values may be sent and summed in bfloat16 or wider, within the bound.
A program may use at most 64 MiB of HBM per device.

v0:
```python
import jax
import jax.numpy as jnp
from jax import lax
from jax.sharding import PartitionSpec as P

LOSS_SCALE = 8.0
NORM_EPS = 1e-06


def body(tokens, w_gate, w_up, w_down, route_ids, route_scores, norm_gain, class_head, targets):
    rows_here, feature_dim = tokens.shape
    top_count = route_ids.shape[1]
    expert_count = lax.axis_size("expert")
    local_experts = w_gate.shape[0]
    experts_all = expert_count * local_experts
    capacity = min(rows_here, rows_here * top_count * 5 // (4 * experts_all))
    route_weight = route_scores / jnp.sum(route_scores, axis=-1, keepdims=True)
    expert_iota = jnp.arange(experts_all, dtype=jnp.int32)
    named_count = jnp.zeros((rows_here, experts_all), jnp.int32)
    for choice_k in range(top_count):
        named_count = named_count + (
            route_ids[:, choice_k][:, None] == expert_iota[None, :]
        ).astype(jnp.int32)
    before = jnp.cumsum(named_count, axis=0) - named_count
    position_cols = []
    for choice_k in range(top_count):
        hit_expert = route_ids[:, choice_k][:, None] == expert_iota[None, :]
        position_cols.append(jnp.sum(jnp.where(hit_expert, before, 0), axis=1))
    position = jnp.stack(position_cols, axis=1)
    slot_index = route_ids * capacity + position
    slot_iota = jnp.arange(experts_all * capacity, dtype=jnp.int32)
    place_rows = jnp.zeros((experts_all * capacity, rows_here), jnp.float32)
    place_weight = jnp.zeros((experts_all * capacity, rows_here), jnp.float32)
    for choice_k in range(top_count):
        slot_hit = slot_iota[:, None] == slot_index[:, choice_k][None, :]
        place_rows = place_rows + slot_hit.astype(jnp.float32)
        place_weight = place_weight + jnp.where(slot_hit, route_weight[:, choice_k][None, :], 0.0)
    place_rows = place_rows.astype(jnp.bfloat16)
    slot_shape = (expert_count, local_experts, capacity, feature_dim)
    outgoing = (
        jnp.dot(place_rows, tokens, preferred_element_type=jnp.float32)
        .astype(jnp.bfloat16)
        .reshape(slot_shape)
    )
    gate_full, up_full, down_full = (
        lax.all_gather(w_gate, "group", axis=1, tiled=True),
        lax.all_gather(w_up, "group", axis=1, tiled=True),
        lax.all_gather(w_down, "group", axis=1, tiled=True),
    )
    incoming = lax.all_to_all(outgoing, "expert", split_axis=0, concat_axis=0, tiled=True)
    gate_list = []
    up_list = []
    hidden_list = []
    for local in range(local_experts):
        expert_rows = incoming[:, local].reshape(-1, feature_dim)
        gate_act = jnp.dot(expert_rows, gate_full[local], preferred_element_type=jnp.float32)
        up_act = jnp.dot(expert_rows, up_full[local], preferred_element_type=jnp.float32)
        hidden = (gate_act * jax.nn.sigmoid(gate_act) * up_act).astype(jnp.bfloat16)
        gate_list.append(gate_act)
        up_list.append(up_act)
        hidden_list.append(hidden)
    out_list = []
    for local in range(local_experts):
        expert_out = jnp.dot(
            hidden_list[local], down_full[local], preferred_element_type=jnp.float32
        ).astype(jnp.bfloat16)
        out_list.append(expert_out.reshape(expert_count, capacity, feature_dim))
    expert_out_all = jnp.stack(out_list, axis=1)
    returned = lax.all_to_all(
        expert_out_all, "expert", split_axis=0, concat_axis=0, tiled=True
    ).reshape(-1, feature_dim)
    picked = jnp.take(returned, slot_index.reshape(-1), axis=0).reshape(
        rows_here, top_count, feature_dim
    )
    moe_out = jnp.einsum("tk,tkd->td", route_weight, picked.astype(jnp.float32))
    residual = tokens.astype(jnp.float32) + moe_out
    inv_rms = lax.rsqrt(jnp.mean(residual * residual, axis=-1, keepdims=True) + NORM_EPS)
    normed = residual * inv_rms * norm_gain
    pooled = jnp.mean(normed, axis=0, keepdims=True).astype(jnp.bfloat16)
    pooled_all = lax.all_gather(pooled, "expert", axis=0, tiled=True)
    logits = jnp.dot(pooled_all, class_head, preferred_element_type=jnp.float32)
    target_rows = targets.reshape(expert_count, -1).astype(jnp.float32)
    logit_grad = (LOSS_SCALE * (jax.nn.sigmoid(logits) - target_rows)).astype(jnp.bfloat16)
    head_part = lax.dot_general(
        pooled_all, logit_grad, (((0,), (0,)), ((), ())), preferred_element_type=jnp.float32
    )
    head_grad = lax.psum(head_part.astype(jnp.bfloat16), "group").astype(jnp.float32)
    pooled_terms = lax.dot_general(
        logit_grad, class_head, (((1,), (1,)), ((), ())), preferred_element_type=jnp.float32
    )
    pooled_grad = lax.psum_scatter(
        pooled_terms.astype(jnp.bfloat16), "expert", scatter_dimension=0, tiled=True
    ).astype(jnp.float32)
    scaled = norm_gain * pooled_grad / rows_here
    cube = inv_rms * inv_rms * inv_rms
    resid_grad = inv_rms * scaled - residual * cube * jnp.mean(
        residual * scaled, axis=-1, keepdims=True
    )
    slot_grad = jnp.dot(
        place_weight,
        resid_grad,
        precision=lax.Precision.HIGHEST,
        preferred_element_type=jnp.float32,
    )
    slot_grad = slot_grad.astype(jnp.bfloat16).reshape(slot_shape)
    grad_in = lax.all_to_all(slot_grad, "expert", split_axis=0, concat_axis=0, tiled=True)
    back_list = []
    for local in range(local_experts):
        grad_rows = grad_in[:, local].reshape(-1, feature_dim)
        gate_act = gate_list[local]
        sigmoid_gate = jax.nn.sigmoid(gate_act)
        down_back = lax.dot_general(
            grad_rows,
            down_full[local],
            (((1,), (1,)), ((), ())),
            preferred_element_type=jnp.float32,
        )
        silu_slope = sigmoid_gate * (1.0 + gate_act * (1.0 - sigmoid_gate))
        gate_grad = (down_back * up_list[local] * silu_slope).astype(jnp.bfloat16)
        up_grad = (down_back * gate_act * sigmoid_gate).astype(jnp.bfloat16)
        input_grad = lax.dot_general(
            gate_grad,
            gate_full[local],
            (((1,), (1,)), ((), ())),
            preferred_element_type=jnp.float32,
        )
        input_grad = input_grad + lax.dot_general(
            up_grad, up_full[local], (((1,), (1,)), ((), ())), preferred_element_type=jnp.float32
        )
        back_list.append(
            input_grad.astype(jnp.bfloat16).reshape(expert_count, capacity, feature_dim)
        )
    input_grad_all = jnp.stack(back_list, axis=1)
    grad_back = lax.all_to_all(
        input_grad_all, "expert", split_axis=0, concat_axis=0, tiled=True
    ).reshape(-1, feature_dim)
    grad_pick = jnp.take(grad_back, slot_index.reshape(-1), axis=0).reshape(
        rows_here, top_count, feature_dim
    )
    token_grad = (resid_grad + jnp.sum(grad_pick.astype(jnp.float32), axis=1)).astype(jnp.bfloat16)
    return (token_grad, head_grad)


def solution(mesh):
    in_specs = (
        P(("rep", "expert", "group"), None),
        P("expert", "group", None),
        P("expert", "group", None),
        P("expert", "group", None),
        P(("rep", "expert", "group"), None),
        P(("rep", "expert", "group"), None),
        P(),
        P(None, "expert"),
        P("rep", "group", "expert"),
    )
    out_specs = (P(("rep", "expert", "group"), None), P("rep", "expert"))
    return jax.shard_map(body, mesh=mesh, in_specs=in_specs, out_specs=out_specs, check_vma=False)
```

profile of v0, /device:TPU:0, one launch (start us, length us, event | category | flops | bytes accessed | tf_op | source)
XLA Modules:
  0.0 371.7 jit_solution(3693473801401391951)
XLA Ops:
  7.2 1.0 slice_bitcast_fusion.41
  9.7 3.5 convolution_convert_fusion.1
  13.2 7.2 %all-to-all-start = ((bf16[8,2,80,1024]{3,2,1,0:T(8,128)(2,1)}), bf16[8,2,80,1024]{3,2,1,0:T(8,128)(2,1)S(1)}, u32[]{:S(2)}, u32[]{:S(2)}) async-start(bf16[8,2,80,1024]{3,2,1,0:T(8,128)(2,1)} %bitcast.142), calls=%async_computation | async-start | bytes 5242880 | tf_op jit(solution)/shard_map/all_to_all | solution.py:50
  22.7 57.3 %all-to-all-done = bf16[8,2,80,1024]{3,2,1,0:T(8,128)(2,1)S(1)} async-done(((bf16[8,2,80,1024]{3,2,1,0:T(8,128)(2,1)}), bf16[8,2,80,1024]{3,2,1,0:T(8,128)(2,1)S(1)}, u32[]{:S(2)}, u32[]{:S(2)}) %all-to-all-start) | async-done | bytes 2621472 | tf_op jit(solution)/shard_map/all_to_all | solution.py:50
  79.9 1.9 fusion.82
  81.8 3.4 fusion.12
  85.2 3.1 fusion.13
  88.3 1.9 fusion.17
  91.1 3.0 convolution_convert_fusion.3
  95.0 1.7 pad_maximum_fusion
  96.7 3.8 %all-to-all-start.1 = ((bf16[8,2,80,1024]{3,2,1,0:T(8,128)(2,1)}), bf16[8,2,80,1024]{3,2,1,0:T(8,128)(2,1)S(1)}, u32[]{:S(2)}, u32[]{:S(2)}) async-start(bf16[8,2,80,1024]{3,2,1,0:T(8,128)(2,1)} %pad_maximum_fusion), calls=%async_computation.1 | async-start | bytes 5242880 | tf_op jit(solution)/shard_map/all_to_all | solution.py:69
  101.5 58.6 %all-to-all-done.1 = bf16[8,2,80,1024]{3,2,1,0:T(8,128)(2,1)S(1)} async-done(((bf16[8,2,80,1024]{3,2,1,0:T(8,128)(2,1)}), bf16[8,2,80,1024]{3,2,1,0:T(8,128)(2,1)S(1)}, u32[]{:S(2)}, u32[]{:S(2)}) %all-to-all-start.1) | async-done | bytes 2621472 | tf_op jit(solution)/shard_map/all_to_all | solution.py:69
  160.1 5.4 %gather_fusion = bf16[1024,1024]{1,0:T(8,128)(2,1)} fusion(bf16[1280,1024]{1,0:T(8,128)(2,1)S(1)} %bitcast.140, s32[1024]{0:T(1024)S(1)} %fusion.71), kind=kCustom, calls=%fused_computation.clone | custom fusion | bytes 4198400 | tf_op jit(solution)/shard_map/jit(_take)/gather | solution.py:72
  165.5 2.4 fusion
  168.3 26.0 %all-gather = bf16[8192]{0:T(1024)(128)(2,1)S(1)} all-gather(bf16[1024]{0:T(1024)(128)(2,1)S(1)} %multiply_convert_fusion.12), channel_id=2, replica_groups=mesh['rep'=2,'expert'=8,'group'=2] {'expert'}, dimensions={0}, use_global_device_ids=true | all-gather | bytes 18432 | tf_op jit(solution)/shard_map/all_gather | solution.py:80
  194.8 33.8 %all-reduce = bf16[8,1024]{1,0:T(8,128)(2,1)S(1)} all-reduce(bf16[8,1024]{1,0:T(8,128)(2,1)S(1)} %convolution_convert_fusion.5), channel_id=3, replica_groups=mesh['rep'=2,'expert'=8,'group'=2] {'expert'}, use_global_device_ids=true, to_apply=%region_12.14.clone | all-reduce | flops 8192 | bytes 32768
  229.4 5.3 %convolution_convert_fusion = bf16[1280,1024]{1,0:T(8,128)(2,1)S(1)} fusion(f32[128]{0:T(128)S(1)} %get-tuple-element.16, f32[128]{0:T(128)S(1)} %get-tuple-element.17, f32[128]{0:T(128)S(1)} %get-tuple-element.18, f32[128]{0:T(128)S(1)} %get-tuple-element.19, f32[128]{0:T(128)S(1)} %get-tuple-element.20, f32[128]{0:T(128)S(1)} %get-tuple-element.21, ...), kind=kOutput, calls=%fused_computation.3 | convolution fusion | flops 2019131392 | bytes 3421696 | tf_op jit(solution)/shard_map/dot_general | solution.py:99
  234.7 51.1 %all_to_all.20 = bf16[8,2,80,1024]{3,2,1,0:T(8,128)(2,1)S(1)} all-to-all(bf16[8,2,80,1024]{3,2,1,0:T(8,128)(2,1)S(1)} %bitcast.143), channel_id=1, replica_groups=mesh['rep'=2,'expert'=8,'group'=2] {'expert'}, dimensions={0} | all-to-all | bytes 5242880 | tf_op jit(solution)/shard_map/all_to_all | solution.py:106
  286.2 1.0 copy-done.14
  288.9 1.0 fusion.11
  290.4 0.9 add_convert_fusion.1
  292.8 1.0 fusion.15
  293.8 0.9 add_convert_fusion
  294.7 1.7 pad_maximum_fusion.1
  296.5 3.7 all-to-all-start.3
  300.2 1.1 convolution_convert_fusion.4
  301.4 22.4 %all-reduce.3.cloned.1.call-done = bf16[1024,250]{1,0:T(8,128)(2,1)} async-done(((bf16[1024,250]{1,0:T(8,128)(2,1)}), bf16[1024,250]{1,0:T(8,128)(2,1)}) %all-reduce.3.cloned.1.call-update) | async-done | bytes 512016 | tf_op jit(solution)/shard_map/psum | solution.py:87
  323.8 2.1 convert_element_type.176
  325.9 30.0 %all-to-all-done.3 = bf16[8,2,80,1024]{3,2,1,0:T(8,128)(2,1)S(1)} async-done(((bf16[8,2,80,1024]{3,2,1,0:T(8,128)(2,1)}), bf16[8,2,80,1024]{3,2,1,0:T(8,128)(2,1)S(1)}, u32[]{:S(2)}, u32[]{:S(2)}) %all-to-all-start.3) | async-done | bytes 2621472 | tf_op jit(solution)/shard_map/all_to_all | solution.py:134
  355.9 5.4 %gather_fusion.1 = bf16[1024,1024]{1,0:T(8,128)(2,1)} fusion(bf16[1280,1024]{1,0:T(8,128)(2,1)S(1)} %bitcast.141, s32[1024]{0:T(1024)S(1)} %fusion.71), kind=kCustom, calls=%fused_computation.1.clone | custom fusion | bytes 4198400 | tf_op jit(solution)/shard_map/jit(_take)/gather | solution.py:137
  361.2 3.0 convert_reduce_fusion
  364.3 0.9 add_convert_fusion.3
  (85 shorter events, 12.1 us)
Async XLA Ops:
  7.2 187.2 %copy-start = (bf16[1024,250]{1,0:T(8,128)(2,1)S(1)}, bf16[1024,250]{1,0:T(8,128)(2,1)}, u32[]{:S(2)}) copy-start(bf16[1024,250]{1,0:T(8,128)(2,1)} %param.18) | copy-start | bytes 1536004
  13.2 66.7 %all-to-all-start = ((bf16[8,2,80,1024]{3,2,1,0:T(8,128)(2,1)}), bf16[8,2,80,1024]{3,2,1,0:T(8,128)(2,1)S(1)}, u32[]{:S(2)}, u32[]{:S(2)}) async-start(bf16[8,2,80,1024]{3,2,1,0:T(8,128)(2,1)} %bitcast.142), calls=%async_computation | async-start | bytes 5242880 | tf_op jit(solution)/shard_map/all_to_all | solution.py:50
  20.4 61.4 %all-gather.5.cloned.1.call-start = ((), (), s32[]{:S(2)}) async-start(), calls=%async_computation.4 | async-start | bytes 2359296 | tf_op jit(solution)/shard_map/all_gather | solution.py:46
  21.2 64.1 %all-gather.7.cloned.1.call-start = ((), (), s32[]{:S(2)}) async-start(), calls=%async_computation.5 | async-start | bytes 2359296 | tf_op jit(solution)/shard_map/all_gather | solution.py:47
  21.9 69.1 %all-gather.9.cloned.1.call-start = ((), (), s32[]{:S(2)}) async-start(), calls=%async_computation.6 | async-start | bytes 2359296 | tf_op jit(solution)/shard_map/all_gather | solution.py:48
  81.8 3.4 copy-start.5
  85.2 3.1 copy-start.4
  85.2 3.1 copy-start.11
  88.3 1.9 copy-start.9
  91.0 3.0 copy-start.16
  91.0 3.0 copy-start.18
  91.1 3.0 copy-start.13
  96.7 4.0 %copy-start.6 = (f32[128,8]{0,1:T(8,128)S(1)}, f32[128,8]{0,1:T(8,128)}, u32[]{:S(2)}) copy-start(f32[128,8]{0,1:T(8,128)} %param.16) | copy-start | bytes 12292
  96.7 4.2 %copy-start.15 = (u32[32]{0:T(128)S(1)}, u32[32]{0:T(128)}, u32[]{:S(2)}) copy-start(u32[32]{0:T(128)} %constant.41) | copy-start | bytes 388
  96.7 63.4 %all-to-all-start.1 = ((bf16[8,2,80,1024]{3,2,1,0:T(8,128)(2,1)}), bf16[8,2,80,1024]{3,2,1,0:T(8,128)(2,1)S(1)}, u32[]{:S(2)}, u32[]{:S(2)}) async-start(bf16[8,2,80,1024]{3,2,1,0:T(8,128)(2,1)} %pad_maximum_fusion), calls=%async_computation.1 | async-start | bytes 5242880 | tf_op jit(solution)/shard_map/all_to_all | solution.py:69
  165.5 2.4 copy-start.3
  165.5 2.6 copy-start.7
  167.9 61.5 %copy-start.1 = (f32[128,1,1024]{2,1,0:T(1,128)}, f32[128,1,1024]{2,1,0:T(1,128)S(1)}, u32[]{:S(2)}) copy-start(f32[128,1,1024]{2,1,0:T(1,128)S(1)} %fusion) | copy-start | bytes 1572868
  167.9 26.4 %copy-start.8 = (s32[8,1,250]{2,1,0:T(1,128)S(1)}, s32[8,1,250]{2,1,0:T(1,128)}, u32[]{:S(2)}) copy-start(s32[8,1,250]{2,1,0:T(1,128)} %param.19) | copy-start | bytes 24004
  285.8 1.4 copy-start.14
  285.8 2.3 copy-start.21
  287.2 1.5 copy-start.10
  287.2 1.7 copy-start.20
  288.9 1.4 copy-start.12
  291.3 1.2 copy-start.17
  291.3 1.5 copy-start.19
  296.5 59.4 %all-to-all-start.3 = ((bf16[8,2,80,1024]{3,2,1,0:T(8,128)(2,1)}), bf16[8,2,80,1024]{3,2,1,0:T(8,128)(2,1)S(1)}, u32[]{:S(2)}, u32[]{:S(2)}) async-start(bf16[8,2,80,1024]{3,2,1,0:T(8,128)(2,1)} %pad_maximum_fusion.1), calls=%async_computation.3 | async-start | bytes 5242880 | tf_op jit(solution)/shard_map/all_to_all | solution.py:134
  300.1 23.6 %all-reduce.3.cloned.1.call-start = ((), (), s32[]{:S(2)}) async-start(), calls=%async_computation.7 | async-start | bytes 1048576 | tf_op jit(solution)/shard_map/psum | solution.py:87
  361.2 3.0 copy-start.2
Sparse Core Ops, SparseCore 0:
  22.8 11.2 all-gather.4
  35.6 10.9 all-gather.6
  48.2 10.9 all-gather.8
  303.6 20.1 all-reduce.2
where the time goes:
time: 372 us
  waiting for transfers between devices  170 us (46%)
  blocking collectives  111 us (30%)
  matrix products  31.4 us (8%)
  local copies, waits for them, and re-layouts  17.9 us (5%)
  starting transfers between devices  14.8 us (4%)
  between operations  14.1 us (4%)
  other arithmetic  12.2 us (3%)
    all_to_all x1, waiting for transfers between devices, body(): lax.all_to_all(expert_out_all, 'expert', split_axis=0, concat_axis=0, til...  58.6 us
    all_to_all x1, waiting for transfers between devices, body(): lax.all_to_all(outgoing, 'expert', split_axis=0, concat_axis=0, tiled=True)  57.3 us
    all_to_all x1, blocking collectives, body(): lax.all_to_all(slot_grad, 'expert', split_axis=0, concat_axis=0, tiled=True)  51.1 us
    unnamed x1, blocking collectives  33.8 us
    all_to_all x1, waiting for transfers between devices, body(): lax.all_to_all(input_grad_all, 'expert', split_axis=0, concat_axis=0, til...  30 us
    all_gather x1, blocking collectives, body(): pooled_all = lax.all_gather(pooled, 'expert', axis=0, tiled=True)  26 us
    psum x1, waiting for transfers between devices, body(): lax.psum(head_part.astype(jnp.bfloat16), 'group').astype(jnp.float32)  22.4 us
  transfers between devices with their start and end apart: 7, of which 4 were waited for; matrix products, arithmetic and copies ran while one was open for 4% of the time, Pallas kernels for 0%

commit v1 on v0

--- a/solution.py
+++ b/solution.py
@@ -77,7 +77,15 @@
     inv_rms = lax.rsqrt(jnp.mean(residual * residual, axis=-1, keepdims=True) + NORM_EPS)
     normed = residual * inv_rms * norm_gain
     pooled = jnp.mean(normed, axis=0, keepdims=True).astype(jnp.bfloat16)
-    pooled_all = lax.all_gather(pooled, "expert", axis=0, tiled=True)
+    n_lanes = jax.lax.axis_size("expert")
+    opened = [(k - 1, k) for k in range(1, n_lanes)] + [(n_lanes - 1, 0)]
+    block_now = pooled
+    trail = [block_now]
+    for _ in range(n_lanes - 1):
+        block_now = jax.lax.ppermute(block_now, "expert", opened)
+        trail += [block_now]
+    r2 = jnp.concatenate([*reversed(trail)], 0)
+    pooled_all = jnp.roll(r2, (jax.lax.axis_index("expert") + 1) * block_now.shape[0], 0)
     logits = jnp.dot(pooled_all, class_head, preferred_element_type=jnp.float32)
     target_rows = targets.reshape(expert_count, -1).astype(jnp.float32)
     logit_grad = (LOSS_SCALE * (jax.nn.sigmoid(logits) - target_rows)).astype(jnp.bfloat16)

time: 372 us -> 384 us (1.032)
  waiting for transfers between devices: 170 us -> 212 us
  blocking collectives: 111 us -> 79.5 us
    ppermute x0 -> x7, waiting for transfers between devices: none -> 42 us  [body(): block_now = jax.lax.ppermute(block_now, 'expert', opened)]
    all_gather x1 -> x0, blocking collectives: 26 us -> none  [body(): pooled_all = lax.all_gather(pooled, 'expert', axis=0, tiled=True)]
    all_to_all x1, blocking collectives: 51.1 us -> 46 us  [body(): lax.all_to_all(slot_grad, 'expert', split_axis=0, concat_axis=0, tiled=True)]
  transfers between devices with their start and end apart: 7 -> 14, of which waited for: 4 -> 11; matrix products, arithmetic and copies ran while one was open for 4% -> 4% of each run, Pallas kernels for 0% -> 0%
where the time goes in v1:
time: 384 us; the launch traced here: 383 us
  waiting for transfers between devices  212 us (55%)
  blocking collectives  79.5 us (21%)
  matrix products  31.5 us (8%)
  local copies, waits for them, and re-layouts  18 us (5%)
  starting transfers between devices  16.3 us (4%)
  between operations  14.1 us (4%)
  other arithmetic  12.2 us (3%)
    all_to_all x1, waiting for transfers between devices, body(): lax.all_to_all(expert_out_all, 'expert', split_axis=0, concat_axis=0, til...  59.2 us
    all_to_all x1, waiting for transfers between devices, body(): lax.all_to_all(outgoing, 'expert', split_axis=0, concat_axis=0, tiled=True)  57.3 us
    all_to_all x1, blocking collectives, body(): lax.all_to_all(slot_grad, 'expert', split_axis=0, concat_axis=0, tiled=True)  46 us
    ppermute x7, waiting for transfers between devices, body(): block_now = jax.lax.ppermute(block_now, 'expert', opened)  42 us
    unnamed x1, blocking collectives  33.4 us
    all_to_all x1, waiting for transfers between devices, body(): lax.all_to_all(input_grad_all, 'expert', split_axis=0, concat_axis=0, til...  28.5 us
    psum x1, waiting for transfers between devices, body(): lax.psum(head_part.astype(jnp.bfloat16), 'group').astype(jnp.float32)  22.4 us
  transfers between devices with their start and end apart: 14, of which 11 were waited for; matrix products, arithmetic and copies ran while one was open for 4% of the time, Pallas kernels for 0%

profile of v1, /device:TPU:0, one launch (start us, length us, event | category | flops | bytes accessed | tf_op | source)
XLA Modules:
  0.0 383.1 jit_solution(7884018732679930614)
XLA Ops:
  9.7 3.6 convolution_convert_fusion.1
  13.2 7.2 %all-to-all-start = ((bf16[8,2,80,1024]{3,2,1,0:T(8,128)(2,1)}), bf16[8,2,80,1024]{3,2,1,0:T(8,128)(2,1)S(1)}, u32[]{:S(2)}, u32[]{:S(2)}) async-start(bf16[8,2,80,1024]{3,2,1,0:T(8,128)(2,1)} %bitcast.140), calls=%async_computation | async-start | bytes 5242880 | tf_op jit(solution)/shard_map/all_to_all | solution.py:50
  22.7 57.3 %all-to-all-done = bf16[8,2,80,1024]{3,2,1,0:T(8,128)(2,1)S(1)} async-done(((bf16[8,2,80,1024]{3,2,1,0:T(8,128)(2,1)}), bf16[8,2,80,1024]{3,2,1,0:T(8,128)(2,1)S(1)}, u32[]{:S(2)}, u32[]{:S(2)}) %all-to-all-start) | async-done | bytes 2621472 | tf_op jit(solution)/shard_map/all_to_all | solution.py:50
  79.9 1.9 fusion.86
  81.8 3.4 fusion.12
  85.3 3.1 fusion.13
  88.4 1.9 fusion.17
  91.2 3.0 convolution_convert_fusion.3
  95.1 1.8 pad_maximum_fusion
  96.8 3.8 all-to-all-start.1
  101.0 59.2 %all-to-all-done.1 = bf16[8,2,80,1024]{3,2,1,0:T(8,128)(2,1)S(1)} async-done(((bf16[8,2,80,1024]{3,2,1,0:T(8,128)(2,1)}), bf16[8,2,80,1024]{3,2,1,0:T(8,128)(2,1)S(1)}, u32[]{:S(2)}, u32[]{:S(2)}) %all-to-all-start.1) | async-done | bytes 2621472 | tf_op jit(solution)/shard_map/all_to_all | solution.py:69
  160.2 5.3 %gather_fusion = bf16[1024,1024]{1,0:T(8,128)(2,1)} fusion(bf16[1280,1024]{1,0:T(8,128)(2,1)S(1)} %bitcast.139, s32[1024]{0:T(1024)S(1)} %fusion.73), kind=kCustom, calls=%fused_computation.clone | custom fusion | bytes 4198400 | tf_op jit(solution)/shard_map/jit(_take)/gather | solution.py:72
  165.6 2.4 fusion
  168.4 1.5 collective-permute-start
  169.9 4.8 %collective-permute-done = bf16[1,1024]{1,0:T(2,128)(2,1)S(1)} collective-permute-done((bf16[1,1024]{1,0:T(2,128)(2,1)S(1)}, bf16[1,1024]{1,0:T(2,128)(2,1)S(1)}, u32[]{:S(2)}, u32[]{:S(2)}) %collective-permute-start) | collective-permute-done | bytes 2080 | tf_op jit(solution)/shard_map/ppermute | solution.py:85
  174.8 6.3 %collective-permute-done.1 = bf16[1,1024]{1,0:T(2,128)(2,1)S(1)} collective-permute-done((bf16[1,1024]{1,0:T(2,128)(2,1)S(1)}, bf16[1,1024]{1,0:T(2,128)(2,1)S(1)}, u32[]{:S(2)}, u32[]{:S(2)}) %collective-permute-start.1) | collective-permute-done | bytes 2080 | tf_op jit(solution)/shard_map/ppermute | solution.py:85
  181.1 6.3 %collective-permute-done.2 = bf16[1,1024]{1,0:T(2,128)(2,1)S(1)} collective-permute-done((bf16[1,1024]{1,0:T(2,128)(2,1)S(1)}, bf16[1,1024]{1,0:T(2,128)(2,1)S(1)}, u32[]{:S(2)}, u32[]{:S(2)}) %collective-permute-start.2) | collective-permute-done | bytes 2080 | tf_op jit(solution)/shard_map/ppermute | solution.py:85
  187.4 6.3 %collective-permute-done.3 = bf16[1,1024]{1,0:T(2,128)(2,1)S(1)} collective-permute-done((bf16[1,1024]{1,0:T(2,128)(2,1)S(1)}, bf16[1,1024]{1,0:T(2,128)(2,1)S(1)}, u32[]{:S(2)}, u32[]{:S(2)}) %collective-permute-start.3) | collective-permute-done | bytes 2080 | tf_op jit(solution)/shard_map/ppermute | solution.py:85
  193.7 6.3 %collective-permute-done.4 = bf16[1,1024]{1,0:T(2,128)(2,1)S(1)} collective-permute-done((bf16[1,1024]{1,0:T(2,128)(2,1)S(1)}, bf16[1,1024]{1,0:T(2,128)(2,1)S(1)}, u32[]{:S(2)}, u32[]{:S(2)}) %collective-permute-start.4) | collective-permute-done | bytes 2080 | tf_op jit(solution)/shard_map/ppermute | solution.py:85
  200.0 6.3 %collective-permute-done.5 = bf16[1,1024]{1,0:T(2,128)(2,1)S(1)} collective-permute-done((bf16[1,1024]{1,0:T(2,128)(2,1)S(1)}, bf16[1,1024]{1,0:T(2,128)(2,1)S(1)}, u32[]{:S(2)}, u32[]{:S(2)}) %collective-permute-start.5) | collective-permute-done | bytes 2080 | tf_op jit(solution)/shard_map/ppermute | solution.py:85
  206.9 5.7 %collective-permute-done.6 = bf16[1,1024]{1,0:T(2,128)(2,1)S(1)} collective-permute-done((bf16[1,1024]{1,0:T(2,128)(2,1)S(1)}, bf16[1,1024]{1,0:T(2,128)(2,1)S(1)}, u32[]{:S(2)}, u32[]{:S(2)}) %collective-permute-start.6) | collective-permute-done | bytes 2080 | tf_op jit(solution)/shard_map/ppermute | solution.py:85
  213.2 33.4 %all-reduce = bf16[8,1024]{1,0:T(8,128)(2,1)S(1)} all-reduce(bf16[8,1024]{1,0:T(8,128)(2,1)S(1)} %convolution_convert_fusion.5), channel_id=2, replica_groups=mesh['rep'=2,'expert'=8,'group'=2] {'expert'}, use_global_device_ids=true, to_apply=%region_12.14.clone | all-reduce | flops 8192 | bytes 32768
  247.4 5.3 %convolution_convert_fusion = bf16[1280,1024]{1,0:T(8,128)(2,1)S(1)} fusion(f32[128]{0:T(128)S(1)} %get-tuple-element.16, f32[128]{0:T(128)S(1)} %get-tuple-element.17, f32[128]{0:T(128)S(1)} %get-tuple-element.18, f32[128]{0:T(128)S(1)} %get-tuple-element.19, f32[128]{0:T(128)S(1)} %get-tuple-element.20, f32[128]{0:T(128)S(1)} %get-tuple-element.21, ...), kind=kOutput, calls=%fused_computation.3 | convolution fusion | flops 2019131392 | bytes 3421696 | tf_op jit(solution)/shard_map/dot_general | solution.py:107
  252.7 46.0 %all_to_all.20 = bf16[8,2,80,1024]{3,2,1,0:T(8,128)(2,1)S(1)} all-to-all(bf16[8,2,80,1024]{3,2,1,0:T(8,128)(2,1)S(1)} %bitcast.141), channel_id=1, replica_groups=mesh['rep'=2,'expert'=8,'group'=2] {'expert'}, dimensions={0} | all-to-all | bytes 5242880 | tf_op jit(solution)/shard_map/all_to_all | solution.py:114
  307.7 1.8 pad_maximum_fusion.1
  309.4 3.6 all-to-all-start.3
  313.1 1.2 convolution_convert_fusion.4
  314.3 22.4 %all-reduce.3.cloned.1.call-done = bf16[1024,250]{1,0:T(8,128)(2,1)} async-done(((bf16[1024,250]{1,0:T(8,128)(2,1)}), bf16[1024,250]{1,0:T(8,128)(2,1)}) %all-reduce.3.cloned.1.call-update) | async-done | bytes 512016 | tf_op jit(solution)/shard_map/psum | solution.py:95
  336.7 2.1 convert_element_type.176
  338.8 28.5 %all-to-all-done.3 = bf16[8,2,80,1024]{3,2,1,0:T(8,128)(2,1)S(1)} async-done(((bf16[8,2,80,1024]{3,2,1,0:T(8,128)(2,1)}), bf16[8,2,80,1024]{3,2,1,0:T(8,128)(2,1)S(1)}, u32[]{:S(2)}, u32[]{:S(2)}) %all-to-all-start.3) | async-done | bytes 2621472 | tf_op jit(solution)/shard_map/all_to_all | solution.py:142
  367.3 5.3 %gather_fusion.1 = bf16[1024,1024]{1,0:T(8,128)(2,1)} fusion(bf16[1280,1024]{1,0:T(8,128)(2,1)S(1)} %bitcast.138, s32[1024]{0:T(1024)S(1)} %fusion.73), kind=kCustom, calls=%fused_computation.1.clone | custom fusion | bytes 4198400 | tf_op jit(solution)/shard_map/jit(_take)/gather | solution.py:145
  372.7 3.0 convert_reduce_fusion
  (99 shorter events, 19.0 us)
Async XLA Ops:
  7.2 205.6 %copy-start = (bf16[1024,250]{1,0:T(8,128)(2,1)S(1)}, bf16[1024,250]{1,0:T(8,128)(2,1)}, u32[]{:S(2)}) copy-start(bf16[1024,250]{1,0:T(8,128)(2,1)} %param.18) | copy-start | bytes 1536004
  13.2 66.7 %all-to-all-start = ((bf16[8,2,80,1024]{3,2,1,0:T(8,128)(2,1)}), bf16[8,2,80,1024]{3,2,1,0:T(8,128)(2,1)S(1)}, u32[]{:S(2)}, u32[]{:S(2)}) async-start(bf16[8,2,80,1024]{3,2,1,0:T(8,128)(2,1)} %bitcast.140), calls=%async_computation | async-start | bytes 5242880 | tf_op jit(solution)/shard_map/all_to_all | solution.py:50
  20.5 61.4 %all-gather.4.cloned.1.call-start = ((), (), s32[]{:S(2)}) async-start(), calls=%async_computation.4 | async-start | bytes 2359296 | tf_op jit(solution)/shard_map/all_gather | solution.py:46
  21.2 64.1 %all-gather.6.cloned.1.call-start = ((), (), s32[]{:S(2)}) async-start(), calls=%async_computation.5 | async-start | bytes 2359296 | tf_op jit(solution)/shard_map/all_gather | solution.py:47
  21.9 69.2 %all-gather.8.cloned.1.call-start = ((), (), s32[]{:S(2)}) async-start(), calls=%async_computation.6 | async-start | bytes 2359296 | tf_op jit(solution)/shard_map/all_gather | solution.py:48
  81.8 3.5 copy-start.5
  85.3 3.1 copy-start.4
  85.3 3.1 copy-start.11
  88.4 1.9 copy-start.9
  91.1 3.0 copy-start.16
  91.1 3.0 copy-start.18
  91.2 3.0 copy-start.13
  96.8 4.0 %copy-start.6 = (f32[128,8]{0,1:T(8,128)S(1)}, f32[128,8]{0,1:T(8,128)}, u32[]{:S(2)}) copy-start(f32[128,8]{0,1:T(8,128)} %param.16) | copy-start | bytes 12292
  96.8 63.4 %all-to-all-start.1 = ((bf16[8,2,80,1024]{3,2,1,0:T(8,128)(2,1)}), bf16[8,2,80,1024]{3,2,1,0:T(8,128)(2,1)S(1)}, u32[]{:S(2)}, u32[]{:S(2)}) async-start(bf16[8,2,80,1024]{3,2,1,0:T(8,128)(2,1)} %pad_maximum_fusion), calls=%async_computation.1 | async-start | bytes 5242880 | tf_op jit(solution)/shard_map/all_to_all | solution.py:69
  165.6 2.4 copy-start.3
  165.6 2.7 copy-start.7
  168.0 79.4 %copy-start.1 = (f32[128,1,1024]{2,1,0:T(1,128)}, f32[128,1,1024]{2,1,0:T(1,128)S(1)}, u32[]{:S(2)}) copy-start(f32[128,1,1024]{2,1,0:T(1,128)S(1)} %fusion) | copy-start | bytes 1572868
  168.0 38.3 %copy-start.15 = (u32[32]{0:T(128)S(1)}, u32[32]{0:T(128)}, u32[]{:S(2)}) copy-start(u32[32]{0:T(128)} %constant.70) | copy-start | bytes 388
  168.0 44.7 %copy-start.8 = (s32[8,1,250]{2,1,0:T(1,128)S(1)}, s32[8,1,250]{2,1,0:T(1,128)}, u32[]{:S(2)}) copy-start(s32[8,1,250]{2,1,0:T(1,128)} %param.19) | copy-start | bytes 24004
  168.4 6.4 %collective-permute-start = (bf16[1,1024]{1,0:T(2,128)(2,1)S(1)}, bf16[1,1024]{1,0:T(2,128)(2,1)S(1)}, u32[]{:S(2)}, u32[]{:S(2)}) collective-permute-start(bf16[1,1024]{1,0:T(2,128)(2,1)S(1)} %convert_element_type.159), channel_id=1, source_target_pairs={{0,2},{2,4},{4,6},{6,8},{8,10},{10,12},{12,14},{14,0},{1,3},{3,5},... | collective-permute-start | bytes 6152 | tf_op jit(solution)/shard_map/ppermute | solution.py:85
  174.8 6.3 %collective-permute-start.1 = (bf16[1,1024]{1,0:T(2,128)(2,1)S(1)}, bf16[1,1024]{1,0:T(2,128)(2,1)S(1)}, u32[]{:S(2)}, u32[]{:S(2)}) collective-permute-start(bf16[1,1024]{1,0:T(2,128)(2,1)S(1)} %collective-permute-done), channel_id=1, source_target_pairs={{0,2},{2,4},{4,6},{6,8},{8,10},{10,12},{12,14},{14,0},{1,3},{3,5},... | collective-permute-start | bytes 6152 | tf_op jit(solution)/shard_map/ppermute | solution.py:85
  181.1 6.3 %collective-permute-start.2 = (bf16[1,1024]{1,0:T(2,128)(2,1)S(1)}, bf16[1,1024]{1,0:T(2,128)(2,1)S(1)}, u32[]{:S(2)}, u32[]{:S(2)}) collective-permute-start(bf16[1,1024]{1,0:T(2,128)(2,1)S(1)} %collective-permute-done.1), channel_id=1, source_target_pairs={{0,2},{2,4},{4,6},{6,8},{8,10},{10,12},{12,14},{14,0},{1,3},{3,5},... | collective-permute-start | bytes 6152 | tf_op jit(solution)/shard_map/ppermute | solution.py:85
  187.4 6.3 %collective-permute-start.3 = (bf16[1,1024]{1,0:T(2,128)(2,1)S(1)}, bf16[1,1024]{1,0:T(2,128)(2,1)S(1)}, u32[]{:S(2)}, u32[]{:S(2)}) collective-permute-start(bf16[1,1024]{1,0:T(2,128)(2,1)S(1)} %collective-permute-done.2), channel_id=1, source_target_pairs={{0,2},{2,4},{4,6},{6,8},{8,10},{10,12},{12,14},{14,0},{1,3},{3,5},... | collective-permute-start | bytes 6152 | tf_op jit(solution)/shard_map/ppermute | solution.py:85
  193.7 6.3 %collective-permute-start.4 = (bf16[1,1024]{1,0:T(2,128)(2,1)S(1)}, bf16[1,1024]{1,0:T(2,128)(2,1)S(1)}, u32[]{:S(2)}, u32[]{:S(2)}) collective-permute-start(bf16[1,1024]{1,0:T(2,128)(2,1)S(1)} %collective-permute-done.3), channel_id=1, source_target_pairs={{0,2},{2,4},{4,6},{6,8},{8,10},{10,12},{12,14},{14,0},{1,3},{3,5},... | collective-permute-start | bytes 6152 | tf_op jit(solution)/shard_map/ppermute | solution.py:85
  200.0 6.3 %collective-permute-start.5 = (bf16[1,1024]{1,0:T(2,128)(2,1)S(1)}, bf16[1,1024]{1,0:T(2,128)(2,1)S(1)}, u32[]{:S(2)}, u32[]{:S(2)}) collective-permute-start(bf16[1,1024]{1,0:T(2,128)(2,1)S(1)} %collective-permute-done.4), channel_id=1, source_target_pairs={{0,2},{2,4},{4,6},{6,8},{8,10},{10,12},{12,14},{14,0},{1,3},{3,5},... | collective-permute-start | bytes 6152 | tf_op jit(solution)/shard_map/ppermute | solution.py:85
  206.3 6.3 %collective-permute-start.6 = (bf16[1,1024]{1,0:T(2,128)(2,1)S(1)}, bf16[1,1024]{1,0:T(2,128)(2,1)S(1)}, u32[]{:S(2)}, u32[]{:S(2)}) collective-permute-start(bf16[1,1024]{1,0:T(2,128)(2,1)S(1)} %collective-permute-done.5), channel_id=1, source_target_pairs={{0,2},{2,4},{4,6},{6,8},{8,10},{10,12},{12,14},{14,0},{1,3},{3,5},... | collective-permute-start | bytes 6152 | tf_op jit(solution)/shard_map/ppermute | solution.py:85
  298.8 2.3 copy-start.21
  300.2 1.7 copy-start.20
  304.2 1.5 copy-start.19
  309.4 57.9 %all-to-all-start.3 = ((bf16[8,2,80,1024]{3,2,1,0:T(8,128)(2,1)}), bf16[8,2,80,1024]{3,2,1,0:T(8,128)(2,1)S(1)}, u32[]{:S(2)}, u32[]{:S(2)}) async-start(bf16[8,2,80,1024]{3,2,1,0:T(8,128)(2,1)} %pad_maximum_fusion.1), calls=%async_computation.3 | async-start | bytes 5242880 | tf_op jit(solution)/shard_map/all_to_all | solution.py:142
  313.1 23.6 %all-reduce.3.cloned.1.call-start = ((), (), s32[]{:S(2)}) async-start(), calls=%async_computation.7 | async-start | bytes 1048576 | tf_op jit(solution)/shard_map/psum | solution.py:95
  372.7 3.0 copy-start.2
  (4 other events, 5.5 us)
Sparse Core Ops, SparseCore 0:
  22.8 11.2 all-gather.3
  35.7 10.9 all-gather.5
  48.2 10.9 all-gather.7
  316.5 20.1 all-reduce.2
